TPU v7x, 32 devices: a whole 2x2x4 slice. The times are simulated.
32 devices in a mesh: sec: 4 (over x, core), col: 8 (over z, y).
Axes of the slice: x: 2, y: 2, z: 4, core: 2. Of those that a mesh axis runs over, the one named last changes fastest.
Arguments:
- rhs: bfloat16 [256, 64, 256], P(('sec', 'col')), may hold values from -6 to 6
- diag_inv: bfloat16 [256, 64, 64], P(('sec', 'col')), may hold values from -0.5 to 0.5
- off_tiles: bfloat16 [256, 16, 64, 64], P(('sec', 'col')), may hold values from -0.1875 to 0.1875
- targets: int32 [256, 16], P(('sec', 'col')), may hold values from 0 to 63, all different within a row
- row_slot: int32 [4, 64], P('sec'), may hold values from 0 to 63, each once within a row
Outputs:
- solution: bfloat16 [256, 64, 256], P(('sec', 'col'))
- handed_on: bfloat16 [256, 64, 256], P(('sec', 'col'))
Inputs may be any that keep to these rules, and one draw needn't show every extreme that they name: The 16 targets of one block are distinct. `row_slot`: each row is a permutation.
All inputs are finite; a program needn't handle non-finite values.
Results may differ from a plain program's by a relative error of at most 0.03.
Values may be sent and summed in bfloat16 or wider, within the bound.
A program may use at most 64 MiB of HBM per device.

v0:
```python
import functools

import jax
import jax.numpy as jnp
from jax import lax
from jax.experimental import pallas as pl
from jax.experimental.pallas import tpu as pltpu
from jax.sharding import PartitionSpec as P

MESH = pl.DeviceIdType.MESH
OWN, MIRROR, OTHER = 0, 1, 2


def low_size(n_col):
    low = 1
    while (2 * low) ** 2 <= n_col:
        low *= 2
    return low


def kernel(
    dims, targets_ref, slot_ref, rhs_hbm, diag_hbm, off_hbm, sol_ref, hand_ref,
    rin, diag_ref, off_ref, pack_own, pack_mirror, idx_vec, idx_ref,
    a_ref, x_ref, inc, send1, recv1, send2, recv2, acc, passed, ret,
    in_sem, fs_sem, fr_sem, s1_sem, r1_sem, s2_sem, r2_sem, sp_sem, rp_sem, sr_sem, rr_sem,
):
    n_sec, n_hi, n_lo = dims
    half = n_sec // 2
    blocks, width = off_hbm.shape[0], off_hbm.shape[2]
    noff = off_hbm.shape[1]
    rows = slot_ref.shape[1]
    lanes = idx_vec.shape[2]
    nc = rin.shape[3]
    size = blocks * width
    pairs = blocks // 2
    sec = lax.axis_index("sec")
    col = lax.axis_index("col")
    plane, place = sec // half, sec % half
    hi, lo = col // n_lo, col % n_lo
    mirror = {"sec": lax.rem(sec + half, n_sec), "col": col}

    def columns_of(which):
        return pl.ds(pl.multiple_of(which * nc, nc), nc)

    loads = [
        pltpu.make_async_copy(off_hbm, off_ref, in_sem.at[0]),
        pltpu.make_async_copy(diag_hbm, diag_ref.at[OWN], in_sem.at[1]),
        pltpu.make_async_copy(rhs_hbm.at[:, :, columns_of(plane)], rin.at[OWN], in_sem.at[2]),
        pltpu.make_async_copy(rhs_hbm.at[:, :, columns_of(1 - plane)], rin.at[OTHER], in_sem.at[3]),
    ]
    for load in loads:
        load.start()

    def lo_peer(o):
        return {"sec": sec, "col": hi * n_lo + lax.rem(lo + o, n_lo)}

    def hi_flip(o):
        value, bit = hi, 1
        while bit < n_hi:
            if o & bit:
                value = value + bit - 2 * bit * ((value // bit) % 2)
            bit *= 2
        return value

    def hi_peer(o):
        return {"sec": sec, "col": hi_flip(o) * n_lo + lo}

    barrier = pltpu.get_barrier_semaphore()
    for o in range(1, n_lo):
        pl.semaphore_signal(barrier, inc=1, device_id=lo_peer(o), device_id_type=MESH)
    for o in range(1, n_hi):
        pl.semaphore_signal(barrier, inc=1, device_id=hi_peer(o), device_id_type=MESH)
    for o in range(1, n_sec):
        pl.semaphore_signal(
            barrier, inc=1, device_id={"sec": lax.rem(sec + o, n_sec), "col": col},
            device_id_type=MESH,
        )

    slot_of_lane = lax.broadcasted_iota(jnp.int32, (1, lanes), 1)
    for k in range(blocks):
        found = jnp.full((1, lanes), noff, jnp.int32)
        for p in range(noff):
            dest = slot_ref[0, targets_ref[k, p]]
            found = jnp.where(slot_of_lane == dest, p, found)
        idx_vec[OWN, k:k + 1, :] = found
    to_scalar = pltpu.make_async_copy(idx_vec.at[OWN], idx_ref.at[OWN], in_sem.at[4])
    to_scalar.start()

    packs = (pack_own, pack_mirror)
    for pack_ref in packs:
        for q in range(pairs):
            pack_ref[q, noff] = jnp.zeros((width, 2 * width), jnp.bfloat16)
    for load in loads:
        load.wait()

    def pack(p, carry):
        for q in range(pairs):
            pack_own[q, p] = jnp.concatenate([off_ref[2 * q, p], off_ref[2 * q + 1, p]], axis=1)
        return carry

    lax.fori_loop(0, noff, pack, 0)
    to_scalar.wait()
    pl.semaphore_wait(barrier, n_lo - 1 + n_hi - 1 + n_sec - 1)

    def factor_copies():
        ends = [
            (idx_vec.at[OWN], idx_vec.at[MIRROR]),
            (diag_ref.at[OWN], diag_ref.at[MIRROR]),
            (rin.at[OTHER], rin.at[MIRROR]),
        ] + [
            (pack_own.at[q, pl.ds(0, noff)], pack_mirror.at[q, pl.ds(0, noff)])
            for q in range(pairs)
        ]
        return [
            pltpu.make_async_remote_copy(
                src_ref=src, dst_ref=dst, send_sem=fs_sem.at[n], recv_sem=fr_sem.at[n],
                device_id=mirror, device_id_type=MESH,
            )
            for n, (src, dst) in enumerate(ends)
        ]

    @pl.when(sec != 0)
    def _():
        for copy in factor_copies():
            copy.start()

    def mirror_factor():
        for copy in factor_copies():
            copy.wait_recv()
        to_scalar = pltpu.make_async_copy(idx_vec.at[MIRROR], idx_ref.at[MIRROR], in_sem.at[5])
        to_scalar.start()
        to_scalar.wait()

    def source(role):
        return lax.rem(role + plane, 2)

    left = lax.broadcasted_iota(jnp.int32, (width, 2 * width), 1) < width

    def build_row(role, src, i):
        pack_ref = packs[src]
        for q in range(pairs):
            a_ref[role, i, :, 2 * q * width:2 * (q + 1) * width] = jnp.where(
                left,
                pack_ref[q, idx_ref[src, 2 * q, i]],
                pack_ref[q, idx_ref[src, 2 * q + 1, i]],
            )

    def build_all(role):
        for src in (OWN, MIRROR):
            @pl.when(source(role) == src)
            def _():
                def step(i, carry):
                    build_row(role, src, i)
                    return carry

                lax.fori_loop(0, rows, step, 0)

    def copy1(j, o, oh):
        return pltpu.make_async_remote_copy(
            src_ref=send1.at[j, o - 1, oh], dst_ref=recv1.at[j, o - 1, oh],
            send_sem=s1_sem.at[j, o - 1, oh], recv_sem=r1_sem.at[j, o - 1, oh],
            device_id=lo_peer(o), device_id_type=MESH,
        )

    def copy2(j, oh):
        return pltpu.make_async_remote_copy(
            src_ref=send2.at[j, oh - 1], dst_ref=recv2.at[j, oh - 1],
            send_sem=s2_sem.at[j, oh - 1], recv_sem=r2_sem.at[j, oh - 1],
            device_id=hi_peer(oh), device_id_type=MESH,
        )

    def copyp(j, to_sec, slot):
        return pltpu.make_async_remote_copy(
            src_ref=passed.at[j], dst_ref=inc.at[slot],
            send_sem=sp_sem.at[j], recv_sem=rp_sem.at[slot],
            device_id={"sec": to_sec, "col": col}, device_id_type=MESH,
        )

    def pass_on(j):
        if j == 0:
            return copyp(0, half + 1, 0)
        more = place + 1 < half
        to_sec = plane * half + jnp.where(more, place + 1, 0)
        if j == 1:
            return copyp(1, to_sec, jnp.where(more, 0, 1))
        return copyp(2, to_sec, 1)

    def give_back(which, j):
        return pltpu.make_async_remote_copy(
            src_ref=(x_ref, passed)[which].at[j], dst_ref=ret.at[which],
            send_sem=sr_sem.at[which], recv_sem=rr_sem.at[which],
            device_id=mirror, device_id_type=MESH,
        )

    order = list(range(n_hi - 1, -1, -1))

    def product(j, oh, o):
        role = max(j - 1, 0)
        dest = hi_flip(oh) * n_lo + lax.rem(lo + o, n_lo)
        if j == 0:
            for r in range(blocks):
                build_row(0, OWN, dest * blocks + r)
        a = a_ref[role, pl.ds(dest * blocks, blocks)].reshape(size, size)
        return jnp.dot(a, x_ref[j], preferred_element_type=jnp.float32)

    def first(j, fresh):
        role = max(j - 1, 0)
        src = source(role)
        which = OTHER if j == 0 else src
        if not fresh:
            copyp(j, sec, role).wait_recv()
        for k in range(blocks):
            part = slice(k * width, (k + 1) * width)
            residual = rin[which, k]
            if not fresh:
                residual = (
                    residual.astype(jnp.float32) - inc[role, part, :].astype(jnp.float32)
                ).astype(jnp.bfloat16)
            x_ref[j, part, :] = jnp.dot(
                diag_ref[src, k], residual, preferred_element_type=jnp.float32
            ).astype(jnp.bfloat16)
        for oh in order:
            for o in range(1, n_lo):
                send1[j, o - 1, oh] = product(j, oh, o).astype(jnp.bfloat16)
                copy1(j, o, oh).start()

    def middle(j):
        for oh in order:
            total = product(j, oh, 0)
            for o in range(1, n_lo):
                copy1(j, o, oh).wait_recv()
                total = total + recv1[j, o - 1, oh].astype(jnp.float32)
            if oh == 0:
                acc[j] = total
            else:
                send2[j, oh - 1] = total.astype(jnp.bfloat16)
                copy2(j, oh).start()

    def last(j):
        total = acc[j]
        for oh in range(1, n_hi):
            copy2(j, oh).wait_recv()
            total = total + recv2[j, oh - 1].astype(jnp.float32)
        passed[j] = total.astype(jnp.bfloat16)
        if j < 2:
            pass_on(j).start()
        else:
            @pl.when(place < half - 1)
            def _():
                pass_on(j).start()

        if j > 0:
            @pl.when(source(j - 1) == MIRROR)
            def _():
                give_back(0, j).start()
                give_back(1, j).start()

    def sent(j):
        for oh in range(n_hi):
            for o in range(1, n_lo):
                copy1(j, o, oh).wait_send()
        for oh in range(1, n_hi):
            copy2(j, oh).wait_send()

    @pl.when(sec == 0)
    def _():
        first(0, True)
        middle(0)
        first(1, True)
        last(0)
        middle(1)
        last(1)
        sent(0)
        sent(1)
        pass_on(0).wait_send()
        pass_on(1).wait_send()

    @pl.when(place > 0)
    def _():
        @pl.when(plane == 1)
        def _():
            mirror_factor()

        build_all(0)
        first(1, False)
        middle(1)
        last(1)
        sent(1)
        pass_on(1).wait_send()

    @pl.when(plane == 0)
    def _():
        mirror_factor()

    build_all(1)
    first(2, False)
    middle(2)
    last(2)
    own = 1 + plane
    sol_ref[:, :, columns_of(plane)] = x_ref[own].reshape(blocks, width, nc)
    hand_ref[:, :, columns_of(plane)] = passed[own].reshape(blocks, width, nc)

    @pl.when(sec == 0)
    def _():
        sol_ref[:, :, nc:2 * nc] = x_ref[0].reshape(blocks, width, nc)
        hand_ref[:, :, nc:2 * nc] = passed[0].reshape(blocks, width, nc)

    @pl.when(sec != 0)
    def _():
        give_back(0, 1).wait_recv()
        sol_ref[:, :, columns_of(1 - plane)] = ret[0].reshape(blocks, width, nc)
        give_back(1, 1).wait_recv()
        hand_ref[:, :, columns_of(1 - plane)] = ret[1].reshape(blocks, width, nc)
        for copy in factor_copies():
            copy.wait_send()

    sent(2)

    @pl.when(place < half - 1)
    def _():
        pass_on(2).wait_send()

    @pl.when(sec != half)
    def _():
        give_back(0, 1).wait_send()
        give_back(1, 1).wait_send()


def shards(n_sec, n_col, rhs, diag_inv, off_tiles, targets, row_slot):
    blocks, width, columns = rhs.shape
    noff = off_tiles.shape[1]
    rows = row_slot.shape[1]
    n_lo = low_size(n_col)
    n_hi = n_col // n_lo
    nc = columns // 2
    size = blocks * width
    pairs = blocks // 2
    lanes = -(-rows // 128) * 128

    vmem = pl.BlockSpec(memory_space=pltpu.VMEM)
    smem = pl.BlockSpec(memory_space=pltpu.SMEM)
    hbm = pl.BlockSpec(memory_space=pl.ANY)
    out = jax.ShapeDtypeStruct((blocks, width, columns), jnp.bfloat16)
    dma = pltpu.SemaphoreType.DMA
    bf16 = jnp.bfloat16
    return pl.pallas_call(
        functools.partial(kernel, (n_sec, n_hi, n_lo)),
        out_shape=(out, out),
        in_specs=[smem, smem, hbm, hbm, hbm],
        out_specs=(vmem, vmem),
        scratch_shapes=[
            pltpu.VMEM((3, blocks, width, nc), bf16),
            pltpu.VMEM((2, blocks, width, width), bf16),
            pltpu.VMEM((blocks, noff, width, width), bf16),
            pltpu.VMEM((pairs, noff + 1, width, 2 * width), bf16),
            pltpu.VMEM((pairs, noff + 1, width, 2 * width), bf16),
            pltpu.VMEM((2, blocks, lanes), jnp.int32),
            pltpu.SMEM((2, blocks, lanes), jnp.int32),
            pltpu.VMEM((2, rows, width, size), bf16),
            pltpu.VMEM((3, size, nc), bf16),
            pltpu.VMEM((2, size, nc), bf16),
            pltpu.VMEM((3, n_lo - 1, n_hi, size, nc), bf16),
            pltpu.VMEM((3, n_lo - 1, n_hi, size, nc), bf16),
            pltpu.VMEM((3, n_hi - 1, size, nc), bf16),
            pltpu.VMEM((3, n_hi - 1, size, nc), bf16),
            pltpu.VMEM((3, size, nc), jnp.float32),
            pltpu.VMEM((3, size, nc), bf16),
            pltpu.VMEM((2, size, nc), bf16),
            dma((6,)),
            dma((3 + pairs,)),
            dma((3 + pairs,)),
            dma((3, n_lo - 1, n_hi)),
            dma((3, n_lo - 1, n_hi)),
            dma((3, n_hi - 1)),
            dma((3, n_hi - 1)),
            dma((3,)),
            dma((2,)),
            dma((2,)),
            dma((2,)),
        ],
        compiler_params=pltpu.CompilerParams(
            collective_id=0, has_side_effects=True, vmem_limit_bytes=60 * 1024 * 1024
        ),
    )(targets, row_slot, rhs, diag_inv, off_tiles)


def solution(mesh):
    return jax.shard_map(
        functools.partial(shards, mesh.shape["sec"], mesh.shape["col"]),
        mesh=mesh,
        in_specs=(
            P(("sec", "col"), None, None),
            P(("sec", "col"), None, None),
            P(("sec", "col"), None, None, None),
            P(("sec", "col"), None),
            P("sec", None),
        ),
        out_specs=(P(("sec", "col"), None, None), P(("sec", "col"), None, None)),
        check_vma=False,
    )
```

profile of v0, /device:TPU:3, one launch (start us, length us, event | category | flops | bytes accessed | tf_op | source)
XLA Modules:
  0.0 75.2 jit_solution(1940328871548487029)
XLA Ops:
  0.6 71.2 %shard_map.68 = (bf16[8,64,256]{2,1,0:T(8,128)(2,1)}, bf16[8,64,256]{2,1,0:T(8,128)(2,1)}) custom-call(s32[8,16]{1,0:T(8,128)} %targets_ref.1, s32[1,64]{1,0:T(1,128)} %slot_ref.1, bf16[8,64,256]{2,1,0:T(8,128)(2,1)} %rhs_hbm.1, bf16[8,64,64]{2,1,0:T(8,128)(2,1)} %diag_hbm.1, bf16[8,16,64,64]{3,2,1,0:T(8,128)(2,1)} %off_hbm.1), custom_call_target="tpu_custom_call" | custom-call | tf_op jit(solution)/shard_map/pallas_call | solution.py:346
  71.9 1.7 %copy.9 = bf16[8,64,256]{2,1,0:T(8,128)(2,1)} copy(bf16[8,64,256]{2,1,0:T(8,128)(2,1)} %get-tuple-element.4) | data formatting | bytes 524288
  73.5 1.7 %copy.10 = bf16[8,64,256]{2,1,0:T(8,128)(2,1)} copy(bf16[8,64,256]{2,1,0:T(8,128)(2,1)} %get-tuple-element.5) | data formatting | bytes 524288
where the time goes:
time: 75.5 us; the launch traced here: 75.2 us
  Pallas kernels  71.2 us (94%)
  local copies, waits for them, and re-layouts  3.34 us (4%)
    pallas_call x1, Pallas kernels, shards(): pl.pallas_call(functools.partial(kernel, (n_sec, n_hi, n_lo)), out_shape=...  71.2 us
    unnamed x2, local copies, waits for them, and re-layouts  3.34 us

commit v1 on v0

--- a/solution.py
+++ b/solution.py
@@ -326,7 +326,7 @@
         give_back(1, 1).wait_send()
 
 
-def shards(n_sec, n_col, rhs, diag_inv, off_tiles, targets, row_slot):
+def mirrored(n_sec, n_col, rhs, diag_inv, off_tiles, targets, row_slot):
     blocks, width, columns = rhs.shape
     noff = off_tiles.shape[1]
     rows = row_slot.shape[1]
@@ -384,6 +384,508 @@
     )(targets, row_slot, rhs, diag_inv, off_tiles)
 
 
+def chains_kernel(
+    dims, targets_ref, slot_ref, rhs_hbm, diag_hbm, off_hbm, sol_ref, hand_ref,
+    rhs_ref, off_ref, pack_0, pack_1, pack_2, pack_3, diag_ref, idx_vec, idx_ref, rin, a_ref, w_ref,
+    send1, recv1, send2, recv2, acc, xs, hs, inc, ret,
+    in_sem, fs_sem, fr_sem, rs_sem, rr_sem, s1_sem, r1_sem, s2_sem, r2_sem, p_sem, gs_sem, gr_sem,
+):
+    n_hi, n_lo = dims
+    blocks, noff, width = off_hbm.shape[:3]
+    lanes = idx_vec.shape[2]
+    pairs = blocks // 2
+    size = blocks * width
+    packed = pairs * width
+    wide = 2 * width
+    sec = lax.axis_index("sec")
+    col = lax.axis_index("col")
+    plane, place = sec // 2, sec % 2
+    hi, lo = col // n_lo, col % n_lo
+    bf16, f32 = jnp.bfloat16, jnp.float32
+
+    own_idx = pltpu.make_async_copy(idx_vec.at[sec], idx_ref.at[sec], in_sem.at[0])
+    load_off = pltpu.make_async_copy(off_hbm, off_ref, in_sem.at[1])
+    load_diag = pltpu.make_async_copy(diag_hbm, diag_ref.at[sec], in_sem.at[2])
+    load_rhs = pltpu.make_async_copy(rhs_hbm, rhs_ref, in_sem.at[3])
+    for load in (load_off, load_diag, load_rhs):
+        load.start()
+
+    def hi_flip(o):
+        value, bit = hi, 1
+        while bit < n_hi:
+            value = value + ((o // bit) % 2) * (bit - 2 * bit * ((value // bit) % 2))
+            bit *= 2
+        return value
+
+    def at_sec(to):
+        return {"sec": to, "col": col}
+
+    lo_peer = {"sec": sec, "col": hi * n_lo + 1 - lo}
+
+    def hi_peer(o):
+        return {"sec": sec, "col": hi_flip(o) * n_lo + lo}
+
+    barrier = pltpu.get_barrier_semaphore()
+    peers = [lo_peer] + [hi_peer(o) for o in range(1, n_hi)]
+    peers += [at_sec(lax.rem(sec + o, 4)) for o in range(1, 4)]
+    for peer in peers:
+        pl.semaphore_signal(barrier, inc=1, device_id=peer, device_id_type=MESH)
+
+    slot_of_lane = lax.broadcasted_iota(jnp.int32, (1, lanes), 1)
+    for k in range(blocks):
+        found = jnp.full((1, lanes), noff, jnp.int32)
+        for p in range(noff):
+            dest = slot_ref[0, targets_ref[k, p]]
+            found = jnp.where(slot_of_lane == dest, p, found)
+        idx_vec[sec, k:k + 1, :] = found
+    own_idx.start()
+    packs = (pack_0, pack_1, pack_2, pack_3)
+    for pack_ref in packs:
+        for q in range(pairs):
+            pack_ref[q, noff] = jnp.zeros((width, wide), bf16)
+
+    left = lax.broadcasted_iota(jnp.int32, (width, wide), 1) < width
+
+    def swap(x):
+        return jnp.concatenate([x[:, width:], x[:, :width]], axis=1)
+
+    load_off.wait()
+
+    def pack_into(pack_ref):
+        def step(p, carry):
+            for q in range(pairs):
+                pack_ref[q, p] = jnp.concatenate([off_ref[2 * q, p], off_ref[2 * q + 1, p]], axis=1)
+            return carry
+
+        lax.fori_loop(0, noff, step, 0)
+
+    for s in range(4):
+        @pl.when(sec == s)
+        def _():
+            pack_into(packs[s])
+
+    load_diag.wait()
+    load_rhs.wait()
+    own_idx.wait()
+    pl.semaphore_wait(barrier, len(peers))
+
+    def factor(s, to, step):
+        ends = [idx_vec.at[s], diag_ref.at[s]]
+        ends += [packs[s].at[q, pl.ds(0, noff)] for q in range(pairs)]
+        return [
+            pltpu.make_async_remote_copy(
+                src_ref=end, dst_ref=end, send_sem=fs_sem.at[step, n], recv_sem=fr_sem.at[s, n],
+                device_id=at_sec(to), device_id_type=MESH,
+            )
+            for n, end in enumerate(ends)
+        ]
+
+    def start(copies):
+        for copy in copies:
+            copy.start()
+
+    def wait_sent(copies):
+        for copy in copies:
+            copy.wait_send()
+
+    def factor_here(s):
+        for copy in factor(s, 0, 0):
+            copy.wait_recv()
+        to_scalar = pltpu.make_async_copy(idx_vec.at[s], idx_ref.at[s], in_sem.at[0])
+        to_scalar.start()
+        to_scalar.wait()
+
+    def rhs_copy(s, chain, to, step):
+        return pltpu.make_async_remote_copy(
+            src_ref=rin.at[s, chain], dst_ref=rin.at[s, chain],
+            send_sem=rs_sem.at[step], recv_sem=rr_sem.at[s, chain // 2],
+            device_id=at_sec(to), device_id_type=MESH,
+        )
+
+    other = plane * 2 + 1 - place
+    for s in range(4):
+        @pl.when(sec == s)
+        def _():
+            start(factor(s, other, 0))
+
+    for m in range(2):
+        part = slice(m * wide, (m + 1) * wide)
+        for q in range(pairs):
+            even, odd = rhs_ref[2 * q, :, part], rhs_ref[2 * q + 1, :, part]
+            rows = slice(q * width, (q + 1) * width)
+            rin[sec, 2 * m, rows] = jnp.where(left, even, swap(odd))
+            rin[sec, 2 * m + 1, rows] = jnp.where(left, swap(even), odd)
+
+    def rhs_sends():
+        first_set = [rhs_copy(sec, 1 - place, other, 0)]
+        return first_set, [rhs_copy(sec, 3 - place, other, 1)], [
+            rhs_copy(sec, 2, 0, 1), rhs_copy(sec, 3, 1, 2),
+        ]
+
+    start(rhs_sends()[0])
+
+    @pl.when(plane == 0)
+    def _():
+        start(rhs_sends()[1])
+
+    @pl.when(plane == 1)
+    def _():
+        start(rhs_sends()[2])
+        for s in (2, 3):
+            @pl.when(sec == s)
+            def _():
+                start(factor(s, place, 1))
+
+    def rhs_here(s, m):
+        rhs_copy(s, 2 * m + place, 0, 0).wait_recv()
+
+    def build(s, d):
+        for r in range(blocks):
+            i = d * blocks + r
+            for q in range(pairs):
+                at = (r % 2) * size + q * wide
+                a_ref[s, d * pairs + r // 2, :, at:at + wide] = jnp.where(
+                    left, packs[s][q, idx_ref[s, 2 * q, i]], packs[s][q, idx_ref[s, 2 * q + 1, i]]
+                )
+
+    def build_range(s, low, high):
+        def step(d, carry):
+            build(s, d)
+            return carry
+
+        lax.fori_loop(low, high, step, 0)
+
+    def copy1(j, oh):
+        return pltpu.make_async_remote_copy(
+            src_ref=send1.at[j, oh], dst_ref=recv1.at[j, oh],
+            send_sem=s1_sem.at[j, oh], recv_sem=r1_sem.at[j, oh],
+            device_id=lo_peer, device_id_type=MESH,
+        )
+
+    def copy2(j, oh):
+        return pltpu.make_async_remote_copy(
+            src_ref=send2.at[j, oh - 1], dst_ref=recv2.at[j, oh - 1],
+            send_sem=s2_sem.at[j, oh - 1], recv_sem=r2_sem.at[j, oh - 1],
+            device_id=hi_peer(oh), device_id_type=MESH,
+        )
+
+    def slot(m, s):
+        return s % 2 if m == 0 else 2 + s
+
+    def give(which, m, s):
+        j = slot(m, s)
+        return pltpu.make_async_remote_copy(
+            src_ref=(xs, hs)[which].at[j], dst_ref=ret.at[which, 2 * m + place],
+            send_sem=gs_sem.at[which, j], recv_sem=gr_sem.at[which, 2 * m + place],
+            device_id=at_sec(s), device_id_type=MESH,
+        )
+
+    def give_out(which, m, s):
+        @pl.when(sec == s)
+        def _():
+            ret[which, 2 * m + place] = (xs, hs)[which][slot(m, s)]
+
+        @pl.when(sec != s)
+        def _():
+            give(which, m, s).start()
+
+    def product(m, s, dest):
+        a = a_ref[s, pl.ds(dest * pairs, pairs)].reshape(packed, 2 * size)
+        return jnp.dot(a, w_ref[m], preferred_element_type=f32)
+
+    def first(m, s, h, fresh=False):
+        j = slot(m, s)
+        for q in range(pairs):
+            rows = slice(q * width, (q + 1) * width)
+            residual = rin[s, 2 * m + place, rows]
+            if h is not None:
+                residual = (residual.astype(f32) - h[rows].astype(f32)).astype(bf16)
+            z = jnp.dot(
+                diag_ref[s, 2 * q:2 * q + 2].reshape(wide, width), residual,
+                preferred_element_type=f32,
+            ).astype(bf16)
+            top, low = z[:width], z[width:]
+            xs[j, rows] = jnp.where(left, top, low)
+            zero = jnp.zeros_like(top)
+            at = q * wide
+            w_ref[m, at:at + width] = jnp.where(left, top, zero)
+            w_ref[m, at + width:at + wide] = jnp.where(left, swap(low), zero)
+            w_ref[m, size + at:size + at + width] = jnp.where(left, zero, swap(top))
+            w_ref[m, size + at + width:size + at + wide] = jnp.where(left, zero, low)
+
+        def step(t, carry):
+            oh = n_hi - 1 - t
+            dest = hi_flip(oh) * n_lo + 1 - lo
+            if fresh:
+                build(s, dest)
+            send1[j, oh] = product(m, s, dest).astype(bf16)
+            copy1(j, oh).start()
+            return carry
+
+        lax.fori_loop(0, n_hi, step, 0)
+        give_out(0, m, s)
+
+    def middle(m, s, fresh=False, also=None):
+        j = slot(m, s)
+
+        def step(t, carry):
+            oh = n_hi - 1 - t
+            dest = hi_flip(oh) * n_lo + lo
+            if fresh:
+                build(s, dest)
+            total = product(m, s, dest)
+            copy1(j, oh).wait_recv()
+            total = total + recv1[j, oh].astype(f32)
+
+            @pl.when(oh > 0)
+            def _():
+                send2[j, oh - 1] = total.astype(bf16)
+                copy2(j, oh).start()
+
+            @pl.when(oh == 0)
+            def _():
+                acc[m] = total
+
+            if also is not None:
+                build(also, 2 * t)
+                build(also, 2 * t + 1)
+            return carry
+
+        lax.fori_loop(0, n_hi, step, 0)
+
+    def last(m, s):
+        j = slot(m, s)
+        total = acc[m]
+        for oh in range(n_hi - 1, 0, -1):
+            copy2(j, oh).wait_recv()
+            total = total + recv2[j, oh - 1].astype(f32)
+        hs[j] = total.astype(bf16)
+
+    def sent(m, s):
+        j = slot(m, s)
+        for oh in range(n_hi):
+            copy1(j, oh).wait_send()
+        for oh in range(1, n_hi):
+            copy2(j, oh).wait_send()
+
+        @pl.when(sec != s)
+        def _():
+            give(0, m, s).wait_send()
+            give(1, m, s).wait_send()
+
+    def pass_on():
+        return pltpu.make_async_remote_copy(
+            src_ref=hs.at[1], dst_ref=inc, send_sem=p_sem.at[0], recv_sem=p_sem.at[1],
+            device_id=at_sec(2 + place), device_id_type=MESH,
+        )
+
+    @pl.when(plane == 0)
+    def _():
+        @pl.when(place == 1)
+        def _():
+            factor_here(0)
+            rhs_here(0, 0)
+            rhs_here(0, 1)
+
+        first(0, 0, None, fresh=True)
+        first(1, 0, None)
+        middle(0, 0, fresh=True)
+
+        @pl.when(place == 0)
+        def _():
+            factor_here(1)
+            rhs_here(1, 0)
+            rhs_here(1, 1)
+
+        middle(1, 0, also=1)
+        last(0, 0)
+        first(0, 1, hs.at[0])
+        give_out(1, 0, 0)
+        last(1, 0)
+        first(1, 1, hs.at[2])
+        give_out(1, 1, 0)
+        middle(0, 1)
+
+        @pl.when(place == 0)
+        def _():
+            factor_here(2)
+            start(factor(2, 1, 1))
+
+        @pl.when(place == 1)
+        def _():
+            factor_here(3)
+            start(factor(3, 0, 1))
+
+        last(0, 1)
+        pass_on().start()
+        give_out(1, 0, 1)
+
+        @pl.when(place == 1)
+        def _():
+            factor_here(2)
+
+        @pl.when(place == 0)
+        def _():
+            factor_here(3)
+
+        middle(1, 1, also=2)
+        last(1, 1)
+        rhs_here(2, 1)
+        first(1, 2, hs.at[3])
+        give_out(1, 1, 1)
+        middle(1, 2, also=3)
+        last(1, 2)
+        rhs_here(3, 1)
+        first(1, 3, hs.at[4])
+        give_out(1, 1, 2)
+        middle(1, 3)
+        last(1, 3)
+        give_out(1, 1, 3)
+        for s in range(2):
+            sent(0, s)
+        for s in range(4):
+            sent(1, s)
+        pass_on().wait_send()
+
+    @pl.when(plane == 1)
+    def _():
+        @pl.when(place == 0)
+        def _():
+            factor_here(3)
+            rhs_here(3, 0)
+
+        @pl.when(place == 1)
+        def _():
+            factor_here(2)
+            rhs_here(2, 0)
+
+        build_range(2, 0, n_hi * n_lo)
+        build_range(3, 0, n_hi * n_lo)
+        pass_on().wait_recv()
+        first(0, 2, inc)
+        middle(0, 2)
+        last(0, 2)
+        first(0, 3, hs.at[0])
+        give_out(1, 0, 2)
+        middle(0, 3)
+        last(0, 3)
+        give_out(1, 0, 3)
+        sent(0, 2)
+        sent(0, 3)
+
+    def returned(which, chain):
+        return pltpu.make_async_remote_copy(
+            src_ref=xs.at[0], dst_ref=ret.at[which, chain],
+            send_sem=gs_sem.at[which, 0], recv_sem=gr_sem.at[which, chain],
+            device_id=at_sec(other), device_id_type=MESH,
+        )
+
+    for which, out in ((0, sol_ref), (1, hand_ref)):
+        for m in range(2):
+            returned(which, 2 * m + 1 - place).wait_recv()
+            if m == 1:
+                @pl.when(plane == 1)
+                def _():
+                    returned(which, 2 + place).wait_recv()
+
+            part = slice(m * wide, (m + 1) * wide)
+            for q in range(pairs):
+                rows = slice(q * width, (q + 1) * width)
+                one, two = ret[which, 2 * m, rows], ret[which, 2 * m + 1, rows]
+                out[2 * q, :, part] = jnp.where(left, one, swap(two))
+                out[2 * q + 1, :, part] = jnp.where(left, swap(one), two)
+
+    wait_sent(factor(0, other, 0))
+    wait_sent(factor(0, other, 1))
+    wait_sent(rhs_sends()[0])
+
+    @pl.when(plane == 0)
+    def _():
+        wait_sent(rhs_sends()[1])
+
+    @pl.when(plane == 1)
+    def _():
+        wait_sent(rhs_sends()[2])
+
+
+def chains(n_col, rhs, diag_inv, off_tiles, targets, row_slot):
+    blocks, width, columns = rhs.shape
+    noff = off_tiles.shape[1]
+    rows = row_slot.shape[1]
+    n_lo = 2
+    n_hi = n_col // n_lo
+    size = blocks * width
+    pairs = blocks // 2
+    packed = pairs * width
+    wide = 2 * width
+    lanes = -(-rows // 128) * 128
+    vmem = pl.BlockSpec(memory_space=pltpu.VMEM)
+    smem = pl.BlockSpec(memory_space=pltpu.SMEM)
+    hbm = pl.BlockSpec(memory_space=pl.ANY)
+    out = jax.ShapeDtypeStruct((blocks, width, columns), jnp.bfloat16)
+    dma = pltpu.SemaphoreType.DMA
+    bf16 = jnp.bfloat16
+    return pl.pallas_call(
+        functools.partial(chains_kernel, (n_hi, n_lo)),
+        out_shape=(out, out),
+        in_specs=[smem, smem, hbm, hbm, hbm],
+        out_specs=(vmem, vmem),
+        scratch_shapes=[
+            pltpu.VMEM((blocks, width, columns), bf16),
+            pltpu.VMEM((blocks, noff, width, width), bf16),
+            pltpu.VMEM((pairs, noff + 1, width, wide), bf16),
+            pltpu.VMEM((pairs, noff + 1, width, wide), bf16),
+            pltpu.VMEM((pairs, noff + 1, width, wide), bf16),
+            pltpu.VMEM((pairs, noff + 1, width, wide), bf16),
+            pltpu.VMEM((4, blocks, width, width), bf16),
+            pltpu.VMEM((4, blocks, lanes), jnp.int32),
+            pltpu.SMEM((4, blocks, lanes), jnp.int32),
+            pltpu.VMEM((4, 4, packed, wide), bf16),
+            pltpu.VMEM((4, rows // 2, width, 2 * size), bf16),
+            pltpu.VMEM((2, 2 * size, wide), bf16),
+            pltpu.VMEM((6, n_hi, packed, wide), bf16),
+            pltpu.VMEM((6, n_hi, packed, wide), bf16),
+            pltpu.VMEM((6, n_hi - 1, packed, wide), bf16),
+            pltpu.VMEM((6, n_hi - 1, packed, wide), bf16),
+            pltpu.VMEM((2, packed, wide), jnp.float32),
+            pltpu.VMEM((6, packed, wide), bf16),
+            pltpu.VMEM((6, packed, wide), bf16),
+            pltpu.VMEM((packed, wide), bf16),
+            pltpu.VMEM((2, 4, packed, wide), bf16),
+            dma((4,)),
+            dma((2, 2 + pairs)),
+            dma((4, 2 + pairs)),
+            dma((3,)),
+            dma((4, 2)),
+            dma((6, n_hi)),
+            dma((6, n_hi)),
+            dma((6, n_hi - 1)),
+            dma((6, n_hi - 1)),
+            dma((2,)),
+            dma((2, 6)),
+            dma((2, 4)),
+        ],
+        compiler_params=pltpu.CompilerParams(
+            collective_id=1, has_side_effects=True, vmem_limit_bytes=60 * 1024 * 1024
+        ),
+    )(targets, row_slot, rhs, diag_inv, off_tiles)
+
+
+def fits_chains(n_sec, n_col, rhs, row_slot):
+    blocks, width, columns = rhs.shape
+    n_hi = n_col // 2
+    return (
+        n_sec == 4 and n_col % 2 == 0 and n_hi & (n_hi - 1) == 0 and columns == 4 * width and width == 64
+        and blocks % 2 == 0 and row_slot.shape[1] == blocks * n_col
+    )
+
+
+def shards(n_sec, n_col, rhs, diag_inv, off_tiles, targets, row_slot):
+    if fits_chains(n_sec, n_col, rhs, row_slot):
+        return chains(n_col, rhs, diag_inv, off_tiles, targets, row_slot)
+    return mirrored(n_sec, n_col, rhs, diag_inv, off_tiles, targets, row_slot)
+
+
 def solution(mesh):
     return jax.shard_map(
         functools.partial(shards, mesh.shape["sec"], mesh.shape["col"]),

time: 75.5 us -> 78.9 us (1.045); the launches traced: 75.2 us -> 77.7 us
  Pallas kernels: 71.2 us -> 73.8 us
    pallas_call x1, Pallas kernels: 71.2 us -> 73.8 us  [chains(): pl.pallas_call(functools.partial(chains_kernel, (n_hi, n_lo)), out_shape=...]
where the time goes in v1:
time: 78.9 us; the launch traced here: 77.7 us
  Pallas kernels  73.8 us (94%)
  local copies, waits for them, and re-layouts  3.34 us (4%)
    pallas_call x1, Pallas kernels, chains(): pl.pallas_call(functools.partial(chains_kernel, (n_hi, n_lo)), out_shape=...  73.8 us
    unnamed x2, local copies, waits for them, and re-layouts  3.34 us

profile of v1, /device:TPU:3, one launch (start us, length us, event | category | flops | bytes accessed | tf_op | source)
XLA Modules:
  0.0 77.7 jit_solution(2724724866649127244)
XLA Ops:
  0.6 73.8 %shard_map.68 = (bf16[8,64,256]{2,1,0:T(8,128)(2,1)}, bf16[8,64,256]{2,1,0:T(8,128)(2,1)}) custom-call(s32[8,16]{1,0:T(8,128)} %targets_ref.1, s32[1,64]{1,0:T(1,128)} %slot_ref.1, bf16[8,64,256]{2,1,0:T(8,128)(2,1)} %rhs_hbm.1, bf16[8,64,64]{2,1,0:T(8,128)(2,1)} %diag_hbm.1, bf16[8,16,64,64]{3,2,1,0:T(8,128)(2,1)} %off_hbm.1), custom_call_target="tpu_custom_call" | custom-call | tf_op jit(solution)/shard_map/pallas_call | solution.py:828
  74.4 1.7 %copy.9 = bf16[8,64,256]{2,1,0:T(8,128)(2,1)} copy(bf16[8,64,256]{2,1,0:T(8,128)(2,1)} %get-tuple-element.4) | data formatting | bytes 524288
  76.1 1.7 %copy.10 = bf16[8,64,256]{2,1,0:T(8,128)(2,1)} copy(bf16[8,64,256]{2,1,0:T(8,128)(2,1)} %get-tuple-element.5) | data formatting | bytes 524288

commit v2 on v1

--- a/solution.py
+++ b/solution.py
@@ -387,7 +387,7 @@
 def chains_kernel(
     dims, targets_ref, slot_ref, rhs_hbm, diag_hbm, off_hbm, sol_ref, hand_ref,
     rhs_ref, off_ref, pack_0, pack_1, pack_2, pack_3, diag_ref, idx_vec, idx_ref, rin, a_ref, w_ref,
-    send1, recv1, send2, recv2, acc, xs, hs, inc, ret,
+    send1, recv1, send2, recv2, acc, xs, hs, ret,
     in_sem, fs_sem, fr_sem, rs_sem, rr_sem, s1_sem, r1_sem, s2_sem, r2_sem, p_sem, gs_sem, gr_sem,
 ):
     n_hi, n_lo = dims
@@ -469,15 +469,18 @@
     own_idx.wait()
     pl.semaphore_wait(barrier, len(peers))
 
-    def factor(s, to, step):
+    every = range(2 + pairs)
+    halves = (range(2 + pairs // 2), range(2 + pairs // 2, 2 + pairs))
+
+    def factor(s, to, step, pieces=every):
         ends = [idx_vec.at[s], diag_ref.at[s]]
         ends += [packs[s].at[q, pl.ds(0, noff)] for q in range(pairs)]
         return [
             pltpu.make_async_remote_copy(
-                src_ref=end, dst_ref=end, send_sem=fs_sem.at[step, n], recv_sem=fr_sem.at[s, n],
+                src_ref=ends[n], dst_ref=ends[n], send_sem=fs_sem.at[step, n], recv_sem=fr_sem.at[s, n],
                 device_id=at_sec(to), device_id_type=MESH,
             )
-            for n, end in enumerate(ends)
+            for n in pieces
         ]
 
     def start(copies):
@@ -488,25 +491,72 @@
         for copy in copies:
             copy.wait_send()
 
+    def to_scalar_memory(s):
+        to_scalar = pltpu.make_async_copy(idx_vec.at[s], idx_ref.at[s], in_sem.at[0])
+        to_scalar.start()
+        to_scalar.wait()
+
     def factor_here(s):
         for copy in factor(s, 0, 0):
             copy.wait_recv()
-        to_scalar = pltpu.make_async_copy(idx_vec.at[s], idx_ref.at[s], in_sem.at[0])
-        to_scalar.start()
-        to_scalar.wait()
-
-    def rhs_copy(s, chain, to, step):
+        to_scalar_memory(s)
+
+    def by_core(act):
+        for core in range(2):
+            @pl.when(place == core)
+            def _():
+                act(core)
+
+    def across(s, act):
+        by_core(lambda core: act(factor(s, 2 - s // 2 * 2 + core, s, halves[core])))
+
+    def arrive(s):
+        def step(core):
+            for copy in factor(s, 0, 0, halves[core]):
+                copy.wait_recv()
+            start(factor(s, s // 2 * -2 + 3 - core, s, halves[core]))
+
+        by_core(step)
+
+    def relayed(s):
+        by_core(lambda core: wait_sent(factor(s, 0, s, halves[core])))
+
+    def arrive_late(s):
+        def step(core):
+            for copy in factor(s, 0, 0, halves[1 - core]):
+                copy.wait_recv()
+
+        by_core(step)
+        to_scalar_memory(s)
+
+    def chain_of(device):
+        return 2 * (1 - device // 2) + device % 2
+
+    mine = chain_of(sec)
+
+    def rhs_copy(s, chain, to, step, slot):
         return pltpu.make_async_remote_copy(
             src_ref=rin.at[s, chain], dst_ref=rin.at[s, chain],
-            send_sem=rs_sem.at[step], recv_sem=rr_sem.at[s, chain // 2],
+            send_sem=rs_sem.at[step], recv_sem=rr_sem.at[slot],
             device_id=at_sec(to), device_id_type=MESH,
         )
+
+    def rhs_sends(s):
+        if s == 0:
+            return [rhs_copy(0, 1, 1, 0, 4), rhs_copy(0, 3, 1, 1, 0)]
+        return [
+            rhs_copy(s, 2 * (1 - to // 2) + to % 2, to, n, s)
+            for n, to in enumerate(to for to in (s ^ 1, s ^ 2, s ^ 3))
+        ]
+
+    def rhs_here(s):
+        rhs_copy(s, mine, 0, 0, s).wait_recv()
 
     other = plane * 2 + 1 - place
     for s in range(4):
         @pl.when(sec == s)
         def _():
-            start(factor(s, other, 0))
+            start(factor(s, s ^ 1, 0))
 
     for m in range(2):
         part = slice(m * wide, (m + 1) * wide)
@@ -516,28 +566,10 @@
             rin[sec, 2 * m, rows] = jnp.where(left, even, swap(odd))
             rin[sec, 2 * m + 1, rows] = jnp.where(left, swap(even), odd)
 
-    def rhs_sends():
-        first_set = [rhs_copy(sec, 1 - place, other, 0)]
-        return first_set, [rhs_copy(sec, 3 - place, other, 1)], [
-            rhs_copy(sec, 2, 0, 1), rhs_copy(sec, 3, 1, 2),
-        ]
-
-    start(rhs_sends()[0])
-
-    @pl.when(plane == 0)
-    def _():
-        start(rhs_sends()[1])
-
-    @pl.when(plane == 1)
-    def _():
-        start(rhs_sends()[2])
-        for s in (2, 3):
-            @pl.when(sec == s)
-            def _():
-                start(factor(s, place, 1))
-
-    def rhs_here(s, m):
-        rhs_copy(s, 2 * m + place, 0, 0).wait_recv()
+    for s in range(4):
+        @pl.when(sec == s)
+        def _():
+            start(rhs_sends(s))
 
     def build(s, d):
         for r in range(blocks):
@@ -569,35 +601,30 @@
             device_id=hi_peer(oh), device_id_type=MESH,
         )
 
-    def slot(m, s):
-        return s % 2 if m == 0 else 2 + s
-
-    def give(which, m, s):
-        j = slot(m, s)
+    def give(which, j, s, chain):
         return pltpu.make_async_remote_copy(
-            src_ref=(xs, hs)[which].at[j], dst_ref=ret.at[which, 2 * m + place],
-            send_sem=gs_sem.at[which, j], recv_sem=gr_sem.at[which, 2 * m + place],
+            src_ref=(xs, hs)[which].at[j], dst_ref=ret.at[which, chain],
+            send_sem=gs_sem.at[which, j], recv_sem=gr_sem.at[which, chain],
             device_id=at_sec(s), device_id_type=MESH,
         )
 
-    def give_out(which, m, s):
+    def give_out(which, j, s, chain):
         @pl.when(sec == s)
         def _():
-            ret[which, 2 * m + place] = (xs, hs)[which][slot(m, s)]
+            ret[which, chain] = (xs, hs)[which][j]
 
         @pl.when(sec != s)
         def _():
-            give(which, m, s).start()
-
-    def product(m, s, dest):
+            give(which, j, s, chain).start()
+
+    def product(s, w, dest):
         a = a_ref[s, pl.ds(dest * pairs, pairs)].reshape(packed, 2 * size)
-        return jnp.dot(a, w_ref[m], preferred_element_type=f32)
-
-    def first(m, s, h, fresh=False):
-        j = slot(m, s)
+        return jnp.dot(a, w_ref[w], preferred_element_type=f32)
+
+    def first(s, j, w, chain, h, fresh=False):
         for q in range(pairs):
             rows = slice(q * width, (q + 1) * width)
-            residual = rin[s, 2 * m + place, rows]
+            residual = rin[s, chain, rows]
             if h is not None:
                 residual = (residual.astype(f32) - h[rows].astype(f32)).astype(bf16)
             z = jnp.dot(
@@ -608,32 +635,31 @@
             xs[j, rows] = jnp.where(left, top, low)
             zero = jnp.zeros_like(top)
             at = q * wide
-            w_ref[m, at:at + width] = jnp.where(left, top, zero)
-            w_ref[m, at + width:at + wide] = jnp.where(left, swap(low), zero)
-            w_ref[m, size + at:size + at + width] = jnp.where(left, zero, swap(top))
-            w_ref[m, size + at + width:size + at + wide] = jnp.where(left, zero, low)
+            w_ref[w, at:at + width] = jnp.where(left, top, zero)
+            w_ref[w, at + width:at + wide] = jnp.where(left, swap(low), zero)
+            w_ref[w, size + at:size + at + width] = jnp.where(left, zero, swap(top))
+            w_ref[w, size + at + width:size + at + wide] = jnp.where(left, zero, low)
 
         def step(t, carry):
             oh = n_hi - 1 - t
             dest = hi_flip(oh) * n_lo + 1 - lo
             if fresh:
                 build(s, dest)
-            send1[j, oh] = product(m, s, dest).astype(bf16)
+            send1[j, oh] = product(s, w, dest).astype(bf16)
             copy1(j, oh).start()
             return carry
 
         lax.fori_loop(0, n_hi, step, 0)
-        give_out(0, m, s)
-
-    def middle(m, s, fresh=False, also=None):
-        j = slot(m, s)
+        give_out(0, j, s, chain)
+
+    def middle(s, j, w, fresh=False, also=None):
 
         def step(t, carry):
             oh = n_hi - 1 - t
             dest = hi_flip(oh) * n_lo + lo
             if fresh:
                 build(s, dest)
-            total = product(m, s, dest)
+            total = product(s, w, dest)
             copy1(j, oh).wait_recv()
             total = total + recv1[j, oh].astype(f32)
 
@@ -644,25 +670,25 @@
 
             @pl.when(oh == 0)
             def _():
-                acc[m] = total
+                acc[w] = total
 
             if also is not None:
-                build(also, 2 * t)
-                build(also, 2 * t + 1)
+                @pl.when(plane == 0)
+                def _():
+                    build(also, 2 * t)
+                    build(also, 2 * t + 1)
             return carry
 
         lax.fori_loop(0, n_hi, step, 0)
 
-    def last(m, s):
-        j = slot(m, s)
-        total = acc[m]
+    def last(j, w):
+        total = acc[w]
         for oh in range(n_hi - 1, 0, -1):
             copy2(j, oh).wait_recv()
             total = total + recv2[j, oh - 1].astype(f32)
         hs[j] = total.astype(bf16)
 
-    def sent(m, s):
-        j = slot(m, s)
+    def sent(j, s):
         for oh in range(n_hi):
             copy1(j, oh).wait_send()
         for oh in range(1, n_hi):
@@ -670,108 +696,88 @@
 
         @pl.when(sec != s)
         def _():
-            give(0, m, s).wait_send()
-            give(1, m, s).wait_send()
+            give(0, j, s, mine).wait_send()
+            give(1, j, s, mine).wait_send()
 
     def pass_on():
         return pltpu.make_async_remote_copy(
-            src_ref=hs.at[1], dst_ref=inc, send_sem=p_sem.at[0], recv_sem=p_sem.at[1],
+            src_ref=hs.at[4], dst_ref=hs.at[0], send_sem=p_sem.at[0], recv_sem=p_sem.at[1],
             device_id=at_sec(2 + place), device_id_type=MESH,
         )
 
+    def here(s):
+        factor_here(s)
+        if s > 0:
+            rhs_here(s)
+
     @pl.when(plane == 0)
     def _():
         @pl.when(place == 1)
         def _():
-            factor_here(0)
-            rhs_here(0, 0)
-            rhs_here(0, 1)
-
-        first(0, 0, None, fresh=True)
-        first(1, 0, None)
-        middle(0, 0, fresh=True)
+            across(1, start)
+            here(0)
+            rhs_copy(0, 1, 0, 0, 4).wait_recv()
+            rhs_copy(0, 3, 0, 0, 0).wait_recv()
+
+        first(0, 4, 0, place, None, fresh=True)
 
         @pl.when(place == 0)
         def _():
-            factor_here(1)
-            rhs_here(1, 0)
-            rhs_here(1, 1)
-
-        middle(1, 0, also=1)
-        last(0, 0)
-        first(0, 1, hs.at[0])
-        give_out(1, 0, 0)
-        last(1, 0)
-        first(1, 1, hs.at[2])
-        give_out(1, 1, 0)
-        middle(0, 1)
-
-        @pl.when(place == 0)
-        def _():
-            factor_here(2)
-            start(factor(2, 1, 1))
-
-        @pl.when(place == 1)
-        def _():
-            factor_here(3)
-            start(factor(3, 0, 1))
-
+            here(1)
+            across(1, start)
+
+        first(0, 0, 1, mine, None)
+        middle(0, 4, 0, fresh=True)
+        middle(0, 0, 1)
+        last(4, 0)
+        pass_on().start()
+        give_out(1, 4, 0, place)
         last(0, 1)
-        pass_on().start()
-        give_out(1, 0, 1)
-
-        @pl.when(place == 1)
-        def _():
-            factor_here(2)
-
-        @pl.when(place == 0)
-        def _():
-            factor_here(3)
-
-        middle(1, 1, also=2)
-        last(1, 1)
-        rhs_here(2, 1)
-        first(1, 2, hs.at[3])
-        give_out(1, 1, 1)
-        middle(1, 2, also=3)
-        last(1, 2)
-        rhs_here(3, 1)
-        first(1, 3, hs.at[4])
-        give_out(1, 1, 2)
-        middle(1, 3)
-        last(1, 3)
-        give_out(1, 1, 3)
-        for s in range(2):
-            sent(0, s)
-        for s in range(4):
-            sent(1, s)
-        pass_on().wait_send()
+        arrive(2)
 
     @pl.when(plane == 1)
     def _():
-        @pl.when(place == 0)
-        def _():
-            factor_here(3)
-            rhs_here(3, 0)
-
-        @pl.when(place == 1)
-        def _():
-            factor_here(2)
-            rhs_here(2, 0)
-
+        for s in (2, 3):
+            @pl.when(sec != s)
+            def _():
+                here(s)
+
+        across(2, start)
         build_range(2, 0, n_hi * n_lo)
         build_range(3, 0, n_hi * n_lo)
+        arrive(1)
+        arrive_late(1)
+        rhs_here(1)
+        across(2, wait_sent)
+        across(3, start)
         pass_on().wait_recv()
-        first(0, 2, inc)
-        middle(0, 2)
-        last(0, 2)
-        first(0, 3, hs.at[0])
-        give_out(1, 0, 2)
-        middle(0, 3)
-        last(0, 3)
-        give_out(1, 0, 3)
-        sent(0, 2)
-        sent(0, 3)
+
+    first(1, 1, 1, mine, hs.at[0], fresh=True)
+
+    @pl.when(plane == 0)
+    def _():
+        give_out(1, 0, 0, mine)
+        arrive_late(2)
+        rhs_here(2)
+
+    middle(1, 1, 1, fresh=True, also=2)
+    last(1, 1)
+    first(2, 2, 1, mine, hs.at[1])
+    give_out(1, 1, 1, mine)
+
+    @pl.when(plane == 0)
+    def _():
+        arrive(3)
+        arrive_late(3)
+        rhs_here(3)
+
+    middle(2, 2, 1, also=3)
+    last(2, 1)
+    first(3, 3, 1, mine, hs.at[2])
+    give_out(1, 2, 2, mine)
+    middle(3, 3, 1)
+    last(3, 1)
+    give_out(1, 3, 3, mine)
 
     def returned(which, chain):
         return pltpu.make_async_remote_copy(
@@ -783,10 +789,10 @@
     for which, out in ((0, sol_ref), (1, hand_ref)):
         for m in range(2):
             returned(which, 2 * m + 1 - place).wait_recv()
-            if m == 1:
-                @pl.when(plane == 1)
-                def _():
-                    returned(which, 2 + place).wait_recv()
+
+            @pl.when((sec != 0) & (plane == m))
+            def _():
+                returned(which, 2 * m + place).wait_recv()
 
             part = slice(m * wide, (m + 1) * wide)
             for q in range(pairs):
@@ -795,17 +801,36 @@
                 out[2 * q, :, part] = jnp.where(left, one, swap(two))
                 out[2 * q + 1, :, part] = jnp.where(left, swap(one), two)
 
+    for s in range(1, 4):
+        sent(s, s)
     wait_sent(factor(0, other, 0))
-    wait_sent(factor(0, other, 1))
-    wait_sent(rhs_sends()[0])
+    for s in range(4):
+        @pl.when(sec == s)
+        def _():
+            wait_sent(rhs_sends(s))
 
     @pl.when(plane == 0)
     def _():
-        wait_sent(rhs_sends()[1])
+        sent(0, 0)
+        for oh in range(n_hi):
+            copy1(4, oh).wait_send()
+        for oh in range(1, n_hi):
+            copy2(4, oh).wait_send()
+
+        @pl.when(sec != 0)
+        def _():
+            give(0, 4, 0, place).wait_send()
+            give(1, 4, 0, place).wait_send()
+
+        pass_on().wait_send()
+        across(1, wait_sent)
+        relayed(2)
+        relayed(3)
 
     @pl.when(plane == 1)
     def _():
-        wait_sent(rhs_sends()[2])
+        across(3, wait_sent)
+        relayed(1)
 
 
 def chains(n_col, rhs, diag_inv, off_tiles, targets, row_slot):
@@ -843,26 +868,25 @@
             pltpu.VMEM((4, 4, packed, wide), bf16),
             pltpu.VMEM((4, rows // 2, width, 2 * size), bf16),
             pltpu.VMEM((2, 2 * size, wide), bf16),
-            pltpu.VMEM((6, n_hi, packed, wide), bf16),
-            pltpu.VMEM((6, n_hi, packed, wide), bf16),
-            pltpu.VMEM((6, n_hi - 1, packed, wide), bf16),
-            pltpu.VMEM((6, n_hi - 1, packed, wide), bf16),
+            pltpu.VMEM((5, n_hi, packed, wide), bf16),
+            pltpu.VMEM((5, n_hi, packed, wide), bf16),
+            pltpu.VMEM((5, n_hi - 1, packed, wide), bf16),
+            pltpu.VMEM((5, n_hi - 1, packed, wide), bf16),
             pltpu.VMEM((2, packed, wide), jnp.float32),
-            pltpu.VMEM((6, packed, wide), bf16),
-            pltpu.VMEM((6, packed, wide), bf16),
-            pltpu.VMEM((packed, wide), bf16),
+            pltpu.VMEM((5, packed, wide), bf16),
+            pltpu.VMEM((5, packed, wide), bf16),
             pltpu.VMEM((2, 4, packed, wide), bf16),
             dma((4,)),
-            dma((2, 2 + pairs)),
+            dma((4, 2 + pairs)),
             dma((4, 2 + pairs)),
             dma((3,)),
-            dma((4, 2)),
-            dma((6, n_hi)),
-            dma((6, n_hi)),
-            dma((6, n_hi - 1)),
-            dma((6, n_hi - 1)),
+            dma((5,)),
+            dma((5, n_hi)),
+            dma((5, n_hi)),
+            dma((5, n_hi - 1)),
+            dma((5, n_hi - 1)),
             dma((2,)),
-            dma((2, 6)),
+            dma((2, 5)),
             dma((2, 4)),
         ],
         compiler_params=pltpu.CompilerParams(

time: 78.9 us -> 69 us (0.87)
  Pallas kernels: 73.8 us -> 64.3 us
    pallas_call x1, Pallas kernels: 73.8 us -> 64.3 us  [chains(): pl.pallas_call(functools.partial(chains_kernel, (n_hi, n_lo)), out_shape=...]
where the time goes in v2:
time: 69 us; the launch traced here: 68.3 us
  Pallas kernels  64.3 us (93%)
  local copies, waits for them, and re-layouts  3.34 us (5%)
    pallas_call x1, Pallas kernels, chains(): pl.pallas_call(functools.partial(chains_kernel, (n_hi, n_lo)), out_shape=...  64.3 us
    unnamed x2, local copies, waits for them, and re-layouts  3.34 us

profile of v2, /device:TPU:3, one launch (start us, length us, event | category | flops | bytes accessed | tf_op | source)
XLA Modules:
  0.0 68.3 jit_solution(14622731767798826930)
XLA Ops:
  0.6 64.3 %shard_map.68 = (bf16[8,64,256]{2,1,0:T(8,128)(2,1)}, bf16[8,64,256]{2,1,0:T(8,128)(2,1)}) custom-call(s32[8,16]{1,0:T(8,128)} %targets_ref.1, s32[1,64]{1,0:T(1,128)} %slot_ref.1, bf16[8,64,256]{2,1,0:T(8,128)(2,1)} %rhs_hbm.1, bf16[8,64,64]{2,1,0:T(8,128)(2,1)} %diag_hbm.1, bf16[8,16,64,64]{3,2,1,0:T(8,128)(2,1)} %off_hbm.1), custom_call_target="tpu_custom_call" | custom-call | tf_op jit(solution)/shard_map/pallas_call | solution.py:853
  65.0 1.7 %copy.9 = bf16[8,64,256]{2,1,0:T(8,128)(2,1)} copy(bf16[8,64,256]{2,1,0:T(8,128)(2,1)} %get-tuple-element.4) | data formatting | bytes 524288
  66.6 1.7 %copy.10 = bf16[8,64,256]{2,1,0:T(8,128)(2,1)} copy(bf16[8,64,256]{2,1,0:T(8,128)(2,1)} %get-tuple-element.5) | data formatting | bytes 524288

commit v3 on v2

--- a/solution.py
+++ b/solution.py
@@ -621,7 +621,7 @@
         a = a_ref[s, pl.ds(dest * pairs, pairs)].reshape(packed, 2 * size)
         return jnp.dot(a, w_ref[w], preferred_element_type=f32)
 
-    def first(s, j, w, chain, h, fresh=False):
+    def first(s, j, w, chain, h, fresh=None):
         for q in range(pairs):
             rows = slice(q * width, (q + 1) * width)
             residual = rin[s, chain, rows]
@@ -643,8 +643,11 @@
         def step(t, carry):
             oh = n_hi - 1 - t
             dest = hi_flip(oh) * n_lo + 1 - lo
-            if fresh:
-                build(s, dest)
+            if fresh is not None:
+                @pl.when(plane <= fresh)
+                def _():
+                    build(s, dest)
+
             send1[j, oh] = product(s, w, dest).astype(bf16)
             copy1(j, oh).start()
             return carry
@@ -652,13 +655,16 @@
         lax.fori_loop(0, n_hi, step, 0)
         give_out(0, j, s, chain)
 
-    def middle(s, j, w, fresh=False, also=None):
+    def middle(s, j, w, fresh=None, also=None):
 
         def step(t, carry):
             oh = n_hi - 1 - t
             dest = hi_flip(oh) * n_lo + lo
-            if fresh:
-                build(s, dest)
+            if fresh is not None:
+                @pl.when(plane <= fresh)
+                def _():
+                    build(s, dest)
+
             total = product(s, w, dest)
             copy1(j, oh).wait_recv()
             total = total + recv1[j, oh].astype(f32)
@@ -719,21 +725,17 @@
             rhs_copy(0, 1, 0, 0, 4).wait_recv()
             rhs_copy(0, 3, 0, 0, 0).wait_recv()
 
-        first(0, 4, 0, place, None, fresh=True)
+        first(0, 0, 1, mine, None, fresh=1)
 
         @pl.when(place == 0)
         def _():
             here(1)
             across(1, start)
 
-        first(0, 0, 1, mine, None)
-        middle(0, 4, 0, fresh=True)
-        middle(0, 0, 1)
-        last(4, 0)
-        pass_on().start()
-        give_out(1, 4, 0, place)
+        first(0, 4, 0, place, None)
+        middle(0, 0, 1, fresh=1)
+        middle(0, 4, 0)
         last(0, 1)
-        arrive(2)
 
     @pl.when(plane == 1)
     def _():
@@ -752,30 +754,47 @@
         across(3, start)
         pass_on().wait_recv()
 
-    first(1, 1, 1, mine, hs.at[0], fresh=True)
+    first(1, 1, 1, mine, hs.at[0], fresh=1)
 
     @pl.when(plane == 0)
     def _():
+        last(4, 0)
+        pass_on().start()
         give_out(1, 0, 0, mine)
+        give_out(1, 4, 0, place)
+
+    middle(1, 1, 1, fresh=1)
+
+    @pl.when(plane == 0)
+    def _():
+        arrive(2)
+
+    last(1, 1)
+
+    @pl.when(plane == 0)
+    def _():
         arrive_late(2)
         rhs_here(2)
 
-    middle(1, 1, 1, fresh=True, also=2)
-    last(1, 1)
-    first(2, 2, 1, mine, hs.at[1])
+    first(2, 2, 1, mine, hs.at[1], fresh=0)
     give_out(1, 1, 1, mine)
 
+    middle(2, 2, 1, fresh=0)
+
     @pl.when(plane == 0)
     def _():
         arrive(3)
+
+    last(2, 1)
+
+    @pl.when(plane == 0)
+    def _():
         arrive_late(3)
         rhs_here(3)
 
-    middle(2, 2, 1, also=3)
-    last(2, 1)
-    first(3, 3, 1, mine, hs.at[2])
+    first(3, 3, 1, mine, hs.at[2], fresh=0)
     give_out(1, 2, 2, mine)
-    middle(3, 3, 1)
+    middle(3, 3, 1, fresh=0)
     last(3, 1)
     give_out(1, 3, 3, mine)
 
@@ -890,7 +909,7 @@
             dma((2, 4)),
         ],
         compiler_params=pltpu.CompilerParams(
-            collective_id=1, has_side_effects=True, vmem_limit_bytes=60 * 1024 * 1024
+            collective_id=1, has_side_effects=True, vmem_limit_bytes=56 * 1024 * 1024
         ),
     )(targets, row_slot, rhs, diag_inv, off_tiles)
 

time: 69 us -> 66.2 us (0.959)
  Pallas kernels: 64.3 us -> 61.9 us
    pallas_call x1, Pallas kernels: 64.3 us -> 61.9 us  [chains(): pl.pallas_call(functools.partial(chains_kernel, (n_hi, n_lo)), out_shape=...]
where the time goes in v3:
time: 66.2 us; the launch traced here: 65.9 us
  Pallas kernels  61.9 us (94%)
  local copies, waits for them, and re-layouts  3.34 us (5%)
    pallas_call x1, Pallas kernels, chains(): pl.pallas_call(functools.partial(chains_kernel, (n_hi, n_lo)), out_shape=...  61.9 us
    unnamed x2, local copies, waits for them, and re-layouts  3.34 us

profile of v3, /device:TPU:3, one launch (start us, length us, event | category | flops | bytes accessed | tf_op | source)
XLA Modules:
  0.0 65.9 jit_solution(16152463264035611476)
XLA Ops:
  0.6 61.9 %shard_map.68 = (bf16[8,64,256]{2,1,0:T(8,128)(2,1)}, bf16[8,64,256]{2,1,0:T(8,128)(2,1)}) custom-call(s32[8,16]{1,0:T(8,128)} %targets_ref.1, s32[1,64]{1,0:T(1,128)} %slot_ref.1, bf16[8,64,256]{2,1,0:T(8,128)(2,1)} %rhs_hbm.1, bf16[8,64,64]{2,1,0:T(8,128)(2,1)} %diag_hbm.1, bf16[8,16,64,64]{3,2,1,0:T(8,128)(2,1)} %off_hbm.1), custom_call_target="tpu_custom_call" | custom-call | tf_op jit(solution)/shard_map/pallas_call | solution.py:872
  62.6 1.7 %copy.9 = bf16[8,64,256]{2,1,0:T(8,128)(2,1)} copy(bf16[8,64,256]{2,1,0:T(8,128)(2,1)} %get-tuple-element.4) | data formatting | bytes 524288
  64.3 1.7 %copy.10 = bf16[8,64,256]{2,1,0:T(8,128)(2,1)} copy(bf16[8,64,256]{2,1,0:T(8,128)(2,1)} %get-tuple-element.5) | data formatting | bytes 524288

commit v4 on v3

--- a/solution.py
+++ b/solution.py
@@ -718,24 +718,30 @@
 
     @pl.when(plane == 0)
     def _():
+        @pl.when(place == 0)
+        def _():
+            first(0, 0, 1, mine, None, fresh=1)
+            here(1)
+            across(1, start)
+            first(0, 4, 0, place, None)
+            middle(0, 0, 1, fresh=1)
+            middle(0, 4, 0)
+            last(0, 1)
+
         @pl.when(place == 1)
         def _():
             across(1, start)
             here(0)
             rhs_copy(0, 1, 0, 0, 4).wait_recv()
             rhs_copy(0, 3, 0, 0, 0).wait_recv()
-
-        first(0, 0, 1, mine, None, fresh=1)
-
-        @pl.when(place == 0)
-        def _():
-            here(1)
-            across(1, start)
-
-        first(0, 4, 0, place, None)
-        middle(0, 0, 1, fresh=1)
-        middle(0, 4, 0)
-        last(0, 1)
+            first(0, 4, 0, place, None, fresh=1)
+            first(0, 0, 1, mine, None)
+            middle(0, 4, 0, fresh=1)
+            middle(0, 0, 1)
+            last(4, 0)
+            pass_on().start()
+            give_out(1, 4, 0, place)
+            last(0, 1)
 
     @pl.when(plane == 1)
     def _():
@@ -758,14 +764,21 @@
 
     @pl.when(plane == 0)
     def _():
-        last(4, 0)
-        pass_on().start()
+        @pl.when(place == 0)
+        def _():
+            last(4, 0)
+            pass_on().start()
+            give_out(1, 4, 0, place)
+
         give_out(1, 0, 0, mine)
-        give_out(1, 4, 0, place)
+
+    @pl.when((plane == 0) & (place == 1))
+    def _():
+        arrive(2)
 
     middle(1, 1, 1, fresh=1)
 
-    @pl.when(plane == 0)
+    @pl.when((plane == 0) & (place == 0))
     def _():
         arrive(2)
 
@@ -779,9 +792,13 @@
     first(2, 2, 1, mine, hs.at[1], fresh=0)
     give_out(1, 1, 1, mine)
 
+    @pl.when((plane == 0) & (place == 1))
+    def _():
+        arrive(3)
+
     middle(2, 2, 1, fresh=0)
 
-    @pl.when(plane == 0)
+    @pl.when((plane == 0) & (place == 0))
     def _():
         arrive(3)
 
@@ -909,9 +926,9 @@
             dma((2, 4)),
         ],
         compiler_params=pltpu.CompilerParams(
-            collective_id=1, has_side_effects=True, vmem_limit_bytes=56 * 1024 * 1024
+            collective_id=1, has_side_effects=True, vmem_limit_bytes=48 * 1024 * 1024
         ),
-    )(targets, row_slot, rhs, diag_inv, off_tiles)
+    )(*[pltpu.with_memory_space_constraint(x, pltpu.MemorySpace.HBM) for x in (targets, row_slot, rhs, diag_inv, off_tiles)])
 
 
 def fits_chains(n_sec, n_col, rhs, row_slot):

time: 66.2 us -> 60.4 us (0.912)
  Pallas kernels: 61.9 us -> 58.1 us
  local copies, waits for them, and re-layouts: 3.34 us -> 1.41 us
    pallas_call x1, Pallas kernels: 61.9 us -> 58.1 us  [chains(): pl.pallas_call(functools.partial(chains_kernel, (n_hi, n_lo)), out_shape=...]
    unnamed x2, local copies, waits for them, and re-layouts: 3.34 us -> 1.41 us
where the time goes in v4:
time: 60.4 us; the launch traced here: 60.2 us
  Pallas kernels  58.1 us (96%)
  local copies, waits for them, and re-layouts  1.41 us (2%)
  between operations  0.64 us (1%)
    pallas_call x1, Pallas kernels, chains(): pl.pallas_call(functools.partial(chains_kernel, (n_hi, n_lo)), out_shape=...  58.1 us
    unnamed x2, local copies, waits for them, and re-layouts  1.41 us

profile of v4, /device:TPU:3, one launch (start us, length us, event | category | flops | bytes accessed | tf_op | source)
XLA Modules:
  0.0 60.2 jit_solution(2609072148568393684)
XLA Ops:
  0.6 58.1 %shard_map.68 = (bf16[8,64,256]{2,1,0:T(8,128)(2,1)S(1)}, bf16[8,64,256]{2,1,0:T(8,128)(2,1)S(1)}) custom-call(s32[8,16]{1,0:T(8,128)} %targets_ref.1, s32[1,64]{1,0:T(1,128)} %slot_ref.1, bf16[8,64,256]{2,1,0:T(8,128)(2,1)} %rhs_hbm.1, bf16[8,64,64]{2,1,0:T(8,128)(2,1)} %diag_hbm.1, bf16[8,16,64,64]{3,2,1,0:T(8,128)(2,1)} %off_hbm.1), custom_call_target="tpu_custom_call" | custom-call | tf_op jit(solution)/shard_map/pallas_call | solution.py:889
  58.8 0.7 %copy.9 = bf16[8,64,256]{2,1,0:T(8,128)(2,1)} copy(bf16[8,64,256]{2,1,0:T(8,128)(2,1)S(1)} %get-tuple-element.4) | data formatting | bytes 524288
  59.5 0.7 %copy.10 = bf16[8,64,256]{2,1,0:T(8,128)(2,1)} copy(bf16[8,64,256]{2,1,0:T(8,128)(2,1)S(1)} %get-tuple-element.5) | data formatting | bytes 524288

commit v5 on v4

--- a/solution.py
+++ b/solution.py
@@ -404,10 +404,15 @@
     bf16, f32 = jnp.bfloat16, jnp.float32
 
     own_idx = pltpu.make_async_copy(idx_vec.at[sec], idx_ref.at[sec], in_sem.at[0])
-    load_off = pltpu.make_async_copy(off_hbm, off_ref, in_sem.at[1])
+    load_off = [
+        pltpu.make_async_copy(
+            off_hbm.at[pl.ds(2 * q, 2)], off_ref.at[pl.ds(2 * q, 2)], in_sem.at[3 + q]
+        )
+        for q in range(pairs)
+    ]
     load_diag = pltpu.make_async_copy(diag_hbm, diag_ref.at[sec], in_sem.at[2])
-    load_rhs = pltpu.make_async_copy(rhs_hbm, rhs_ref, in_sem.at[3])
-    for load in (load_off, load_diag, load_rhs):
+    load_rhs = pltpu.make_async_copy(rhs_hbm, rhs_ref, in_sem.at[1])
+    for load in (*load_off, load_diag, load_rhs):
         load.start()
 
     def hi_flip(o):
@@ -449,15 +454,15 @@
     def swap(x):
         return jnp.concatenate([x[:, width:], x[:, :width]], axis=1)
 
-    load_off.wait()
-
     def pack_into(pack_ref):
-        def step(p, carry):
-            for q in range(pairs):
+        for q in range(pairs):
+            load_off[q].wait()
+
+            def step(p, carry):
                 pack_ref[q, p] = jnp.concatenate([off_ref[2 * q, p], off_ref[2 * q + 1, p]], axis=1)
-            return carry
-
-        lax.fori_loop(0, noff, step, 0)
+                return carry
+
+            lax.fori_loop(0, noff, step, 0, unroll=4)
 
     for s in range(4):
         @pl.when(sec == s)
@@ -467,10 +472,21 @@
     load_diag.wait()
     load_rhs.wait()
     own_idx.wait()
+    for m in range(2):
+        part = slice(m * wide, (m + 1) * wide)
+        for q in range(pairs):
+            even, odd = rhs_ref[2 * q, :, part], rhs_ref[2 * q + 1, :, part]
+            rows = slice(q * width, (q + 1) * width)
+            rin[sec, 2 * m, rows] = jnp.where(left, even, swap(odd))
+            rin[sec, 2 * m + 1, rows] = jnp.where(left, swap(even), odd)
+
     pl.semaphore_wait(barrier, len(peers))
 
     every = range(2 + pairs)
-    halves = (range(2 + pairs // 2), range(2 + pairs // 2, 2 + pairs))
+    def shares(s):
+        cut = 3 if s == 1 else 2 + pairs // 2
+        return range(cut), range(cut, 2 + pairs)
+
 
     def factor(s, to, step, pieces=every):
         ends = [idx_vec.at[s], diag_ref.at[s]]
@@ -508,22 +524,23 @@
                 act(core)
 
     def across(s, act):
-        by_core(lambda core: act(factor(s, 2 - s // 2 * 2 + core, s, halves[core])))
+        by_core(lambda core: act(factor(s, 2 - s // 2 * 2 + core, s, shares(s)[core])))
 
     def arrive(s):
         def step(core):
-            for copy in factor(s, 0, 0, halves[core]):
-                copy.wait_recv()
-            start(factor(s, s // 2 * -2 + 3 - core, s, halves[core]))
+            onward = factor(s, s // 2 * -2 + 3 - core, s, shares(s)[core])
+            for here_now, copy in zip(factor(s, 0, 0, shares(s)[core]), onward):
+                here_now.wait_recv()
+                copy.start()
 
         by_core(step)
 
     def relayed(s):
-        by_core(lambda core: wait_sent(factor(s, 0, s, halves[core])))
+        by_core(lambda core: wait_sent(factor(s, 0, s, shares(s)[core])))
 
     def arrive_late(s):
         def step(core):
-            for copy in factor(s, 0, 0, halves[1 - core]):
+            for copy in factor(s, 0, 0, shares(s)[1 - core]):
                 copy.wait_recv()
 
         by_core(step)
@@ -557,14 +574,6 @@
         @pl.when(sec == s)
         def _():
             start(factor(s, s ^ 1, 0))
-
-    for m in range(2):
-        part = slice(m * wide, (m + 1) * wide)
-        for q in range(pairs):
-            even, odd = rhs_ref[2 * q, :, part], rhs_ref[2 * q + 1, :, part]
-            rows = slice(q * width, (q + 1) * width)
-            rin[sec, 2 * m, rows] = jnp.where(left, even, swap(odd))
-            rin[sec, 2 * m + 1, rows] = jnp.where(left, swap(even), odd)
 
     for s in range(4):
         @pl.when(sec == s)
@@ -721,9 +730,9 @@
         @pl.when(place == 0)
         def _():
             first(0, 0, 1, mine, None, fresh=1)
+            first(0, 4, 0, place, None)
             here(1)
             across(1, start)
-            first(0, 4, 0, place, None)
             middle(0, 0, 1, fresh=1)
             middle(0, 4, 0)
             last(0, 1)
@@ -745,12 +754,16 @@
 
     @pl.when(plane == 1)
     def _():
-        for s in (2, 3):
-            @pl.when(sec != s)
-            def _():
-                here(s)
-
-        across(2, start)
+        @pl.when(place == 0)
+        def _():
+            across(2, start)
+            here(3)
+
+        @pl.when(place == 1)
+        def _():
+            here(2)
+            across(2, start)
+
         build_range(2, 0, n_hi * n_lo)
         build_range(3, 0, n_hi * n_lo)
         arrive(1)
@@ -809,12 +822,6 @@
         arrive_late(3)
         rhs_here(3)
 
-    first(3, 3, 1, mine, hs.at[2], fresh=0)
-    give_out(1, 2, 2, mine)
-    middle(3, 3, 1, fresh=0)
-    last(3, 1)
-    give_out(1, 3, 3, mine)
-
     def returned(which, chain):
         return pltpu.make_async_remote_copy(
             src_ref=xs.at[0], dst_ref=ret.at[which, chain],
@@ -822,7 +829,7 @@
             device_id=at_sec(other), device_id_type=MESH,
         )
 
-    for which, out in ((0, sol_ref), (1, hand_ref)):
+    def assemble(which, out):
         for m in range(2):
             returned(which, 2 * m + 1 - place).wait_recv()
 
@@ -837,8 +844,9 @@
                 out[2 * q, :, part] = jnp.where(left, one, swap(two))
                 out[2 * q + 1, :, part] = jnp.where(left, swap(one), two)
 
-    for s in range(1, 4):
-        sent(s, s)
+    first(3, 3, 1, mine, hs.at[2], fresh=0)
+    give_out(1, 2, 2, mine)
+    sent(1, 1)
     wait_sent(factor(0, other, 0))
     for s in range(4):
         @pl.when(sec == s)
@@ -867,6 +875,14 @@
     def _():
         across(3, wait_sent)
         relayed(1)
+
+    middle(3, 3, 1, fresh=0)
+    assemble(0, sol_ref)
+    sent(2, 2)
+    last(3, 1)
+    give_out(1, 3, 3, mine)
+    assemble(1, hand_ref)
+    sent(3, 3)
 
 
 def chains(n_col, rhs, diag_inv, off_tiles, targets, row_slot):
@@ -912,7 +928,7 @@
             pltpu.VMEM((5, packed, wide), bf16),
             pltpu.VMEM((5, packed, wide), bf16),
             pltpu.VMEM((2, 4, packed, wide), bf16),
-            dma((4,)),
+            dma((3 + pairs,)),
             dma((4, 2 + pairs)),
             dma((4, 2 + pairs)),
             dma((3,)),

time: 60.4 us -> 59.2 us (0.980)
  Pallas kernels: 58.1 us -> 56.9 us
    pallas_call x1, Pallas kernels: 58.1 us -> 56.9 us  [chains(): pl.pallas_call(functools.partial(chains_kernel, (n_hi, n_lo)), out_shape=...]
where the time goes in v5:
time: 59.2 us; the launch traced here: 59 us
  Pallas kernels  56.9 us (96%)
  local copies, waits for them, and re-layouts  1.41 us (2%)
  between operations  0.64 us (1%)
    pallas_call x1, Pallas kernels, chains(): pl.pallas_call(functools.partial(chains_kernel, (n_hi, n_lo)), out_shape=...  56.9 us
    unnamed x2, local copies, waits for them, and re-layouts  1.41 us

profile of v5, /device:TPU:3, one launch (start us, length us, event | category | flops | bytes accessed | tf_op | source)
XLA Modules:
  0.0 59.0 jit_solution(18203902663774218193)
XLA Ops:
  0.6 56.9 %shard_map.68 = (bf16[8,64,256]{2,1,0:T(8,128)(2,1)S(1)}, bf16[8,64,256]{2,1,0:T(8,128)(2,1)S(1)}) custom-call(s32[8,16]{1,0:T(8,128)} %targets_ref.1, s32[1,64]{1,0:T(1,128)} %slot_ref.1, bf16[8,64,256]{2,1,0:T(8,128)(2,1)} %rhs_hbm.1, bf16[8,64,64]{2,1,0:T(8,128)(2,1)} %diag_hbm.1, bf16[8,16,64,64]{3,2,1,0:T(8,128)(2,1)} %off_hbm.1), custom_call_target="tpu_custom_call" | custom-call | tf_op jit(solution)/shard_map/pallas_call | solution.py:905
  57.5 0.7 %copy.9 = bf16[8,64,256]{2,1,0:T(8,128)(2,1)} copy(bf16[8,64,256]{2,1,0:T(8,128)(2,1)S(1)} %get-tuple-element.4) | data formatting | bytes 524288
  58.3 0.7 %copy.10 = bf16[8,64,256]{2,1,0:T(8,128)(2,1)} copy(bf16[8,64,256]{2,1,0:T(8,128)(2,1)S(1)} %get-tuple-element.5) | data formatting | bytes 524288

commit v6 on v5

--- a/solution.py
+++ b/solution.py
@@ -661,7 +661,7 @@
             copy1(j, oh).start()
             return carry
 
-        lax.fori_loop(0, n_hi, step, 0)
+        lax.fori_loop(0, n_hi, step, 0, unroll=True)
         give_out(0, j, s, chain)
 
     def middle(s, j, w, fresh=None, also=None):
@@ -694,7 +694,7 @@
                     build(also, 2 * t + 1)
             return carry
 
-        lax.fori_loop(0, n_hi, step, 0)
+        lax.fori_loop(0, n_hi, step, 0, unroll=True)
 
     def last(j, w):
         total = acc[w]
@@ -769,7 +769,6 @@
         arrive(1)
         arrive_late(1)
         rhs_here(1)
-        across(2, wait_sent)
         across(3, start)
         pass_on().wait_recv()
 
@@ -873,6 +872,7 @@
 
     @pl.when(plane == 1)
     def _():
+        across(2, wait_sent)
         across(3, wait_sent)
         relayed(1)
 

time: 59.2 us -> 59 us (level)
  no operation moved by 1% of the time
where the time goes in v6:
time: 59 us; the launch traced here: 58.7 us
  Pallas kernels  56.6 us (96%)
  local copies, waits for them, and re-layouts  1.41 us (2%)
  between operations  0.64 us (1%)
    pallas_call x1, Pallas kernels, chains(): pl.pallas_call(functools.partial(chains_kernel, (n_hi, n_lo)), out_shape=...  56.6 us
    unnamed x2, local copies, waits for them, and re-layouts  1.41 us

profile of v6, /device:TPU:3, one launch (start us, length us, event | category | flops | bytes accessed | tf_op | source)
XLA Modules:
  0.0 58.7 jit_solution(11740885235287954335)
XLA Ops:
  0.6 56.6 %shard_map.68 = (bf16[8,64,256]{2,1,0:T(8,128)(2,1)S(1)}, bf16[8,64,256]{2,1,0:T(8,128)(2,1)S(1)}) custom-call(s32[8,16]{1,0:T(8,128)} %targets_ref.1, s32[1,64]{1,0:T(1,128)} %slot_ref.1, bf16[8,64,256]{2,1,0:T(8,128)(2,1)} %rhs_hbm.1, bf16[8,64,64]{2,1,0:T(8,128)(2,1)} %diag_hbm.1, bf16[8,16,64,64]{3,2,1,0:T(8,128)(2,1)} %off_hbm.1), custom_call_target="tpu_custom_call" | custom-call | tf_op jit(solution)/shard_map/pallas_call | solution.py:905
  57.3 0.7 %copy.9 = bf16[8,64,256]{2,1,0:T(8,128)(2,1)} copy(bf16[8,64,256]{2,1,0:T(8,128)(2,1)S(1)} %get-tuple-element.4) | data formatting | bytes 524288
  58.0 0.7 %copy.10 = bf16[8,64,256]{2,1,0:T(8,128)(2,1)} copy(bf16[8,64,256]{2,1,0:T(8,128)(2,1)S(1)} %get-tuple-element.5) | data formatting | bytes 524288

commit v7 on v5

--- a/solution.py
+++ b/solution.py
@@ -746,10 +746,10 @@
             first(0, 4, 0, place, None, fresh=1)
             first(0, 0, 1, mine, None)
             middle(0, 4, 0, fresh=1)
-            middle(0, 0, 1)
             last(4, 0)
             pass_on().start()
             give_out(1, 4, 0, place)
+            middle(0, 0, 1)
             last(0, 1)
 
     @pl.when(plane == 1)

time: 59.2 us -> 59.7 us (level)
  the two profiles are of different devices: /device:TPU:3 before, /device:TPU:15 now
where the time goes in v7:
time: 59.7 us; the launch traced here: 59.5 us
  Pallas kernels  57.4 us (96%)
  local copies, waits for them, and re-layouts  1.41 us (2%)
  between operations  0.64 us (1%)
    pallas_call x1, Pallas kernels, chains(): pl.pallas_call(functools.partial(chains_kernel, (n_hi, n_lo)), out_shape=...  57.4 us
    unnamed x2, local copies, waits for them, and re-layouts  1.41 us

profile of v7, /device:TPU:15, one launch (start us, length us, event | category | flops | bytes accessed | tf_op | source)
XLA Modules:
  0.0 59.5 jit_solution(1469017764188141657)
XLA Ops:
  0.6 57.4 %shard_map.68 = (bf16[8,64,256]{2,1,0:T(8,128)(2,1)S(1)}, bf16[8,64,256]{2,1,0:T(8,128)(2,1)S(1)}) custom-call(s32[8,16]{1,0:T(8,128)} %targets_ref.1, s32[1,64]{1,0:T(1,128)} %slot_ref.1, bf16[8,64,256]{2,1,0:T(8,128)(2,1)} %rhs_hbm.1, bf16[8,64,64]{2,1,0:T(8,128)(2,1)} %diag_hbm.1, bf16[8,16,64,64]{3,2,1,0:T(8,128)(2,1)} %off_hbm.1), custom_call_target="tpu_custom_call" | custom-call | tf_op jit(solution)/shard_map/pallas_call | solution.py:905
  58.1 0.7 %copy.9 = bf16[8,64,256]{2,1,0:T(8,128)(2,1)} copy(bf16[8,64,256]{2,1,0:T(8,128)(2,1)S(1)} %get-tuple-element.4) | data formatting | bytes 524288
  58.8 0.7 %copy.10 = bf16[8,64,256]{2,1,0:T(8,128)(2,1)} copy(bf16[8,64,256]{2,1,0:T(8,128)(2,1)S(1)} %get-tuple-element.5) | data formatting | bytes 524288
